TPU v7x, 256 devices: a whole 4x4x8 slice. The times are simulated.
256 devices in a mesh: expert: 8 (over x, core), dp: 32 (over y, z).
Axes of the slice: x: 4, y: 4, z: 8, core: 2. Of those that a mesh axis runs over, the one named last changes fastest.
Arguments:
- tokens: bfloat16 [32768, 1664], P(('expert', 'dp')), may hold values from -6 to 6
- expert_ids: int32 [32768, 2], P(('expert', 'dp')), may hold values from 0 to 15, as said below
- slot_ids: int32 [32768, 2], P(('expert', 'dp')), may hold values from 0 to 3, as said below
- dropped: int32 [32768, 2], P(('expert', 'dp')), may hold values from 0 to 1, as said below
- gates: float32 [32768, 2], P(('expert', 'dp')), may hold values from 0.1 to 1
- w_in: bfloat16 [16, 1664, 8192], P('expert', None, 'dp'), may hold values from -0.15625 to 0.15625
- w_out: bfloat16 [16, 8192, 1664], P('expert', 'dp'), may hold values from -0.0625 to 0.0625
- out_grad: bfloat16 [32768, 1664], P(('expert', 'dp')), may hold values from -6 to 6
Outputs:
- mixed: bfloat16 [32768, 1664], P(('expert', 'dp'))
- tok_grad: bfloat16 [32768, 1664], P(('expert', 'dp'))
- gate_grad: float32 [32768, 2], P(('expert', 'dp'))
- w_in_grad: float32 [16, 1664, 8192], P('expert', None, 'dp')
- w_out_grad: float32 [16, 8192, 1664], P('expert', 'dp')
Inputs may be any that keep to these rules, and one draw needn't show every extreme that they name: `expert_ids`: the two experts of a token differ. `slot_ids`: choices are ranked in each block of 128 tokens by batch priority, all first choices before all second choices; a choice's slot is the number of higher-ranked choices of the same block to the same expert; it is dropped where that number is 4 or more, and its slot is then 0. Kept choices of one expert in one block have distinct slots. In every draw one expert is the first choice of at least 5 tokens of every block. `dropped`: 1 exactly where the slot count described for slot_ids reaches 4.
All inputs are finite; a program needn't handle non-finite values.
Results may differ from a plain program's by a relative error of at most 0.039.
Values may be sent and summed in bfloat16 or wider, within the bound.
A program may use at most 128 MiB of HBM per device.

v0:
```python
import jax
import jax.numpy as jnp
from jax import lax
from jax.sharding import PartitionSpec as P

CAP = 4


inv_root_two = 0.7071067811865476
inv_root_two_pi = 0.3989422804014327


def gelu_exact(value):
    return 0.5 * value * (1.0 + lax.erf(value * inv_root_two))


def gelu_slope(value):
    return (
        0.5 * (1.0 + lax.erf(value * inv_root_two))
        + value * jnp.exp(-0.5 * value * value) * inv_root_two_pi
    )


def spread(buffer):
    grouped = lax.all_gather(buffer[None], "dp", axis=0, tiled=True)
    return lax.all_to_all(grouped, "expert", split_axis=1, concat_axis=1, tiled=True)


def collect(term_fn):
    summed = lax.psum_scatter(
        term_fn(jnp.int32(0), 1 * lax.axis_size("dp")).astype(jnp.bfloat16),
        "dp",
        scatter_dimension=0,
        tiled=True,
    ).astype(jnp.float32)
    return lax.all_to_all(
        summed[0].astype(jnp.bfloat16), "expert", split_axis=0, concat_axis=0, tiled=True
    )


def per_device(tokens, expert_ids, slot_ids, dropped, gates, w_in, w_out, out_grad):
    n_expert = lax.axis_size("expert")
    exp_local = w_in.shape[0]
    width = tokens.shape[1]
    experts_all = n_expert * exp_local
    capacity = CAP
    columns = experts_all * capacity
    target = expert_ids * capacity + slot_ids
    keep = dropped == 0
    column_ids = lax.broadcasted_iota(jnp.int32, (1, 1, columns), 2)
    select = ((target[:, :, None] == column_ids) & keep[:, :, None]).astype(jnp.float32)
    select_half = select.astype(jnp.bfloat16)
    shape_slots = (n_expert, exp_local, capacity, width)
    send_rows = jnp.einsum("tkj,td->jd", select_half, tokens, preferred_element_type=jnp.float32)
    rows = spread(send_rows.astype(jnp.bfloat16).reshape(shape_slots))
    pre = jnp.einsum("pqxcd,xdf->pqxcf", rows, w_in, preferred_element_type=jnp.float32)
    hidden = gelu_exact(pre).astype(jnp.bfloat16)

    def output_term(start, count):
        return jnp.einsum("pqxcf,xfd->pqxcd", hidden, w_out, preferred_element_type=jnp.float32)

    returned = collect(output_term).reshape(columns, width)
    picked = jnp.einsum("tkj,jd->tkd", select_half, returned, preferred_element_type=jnp.float32)
    mixed = jnp.sum(gates[:, :, None] * picked, axis=1).astype(jnp.bfloat16)
    grad_wide = out_grad.astype(jnp.float32)
    gate_grad = jnp.sum(picked * grad_wide[:, None, :], axis=-1)
    scaled = gates[:, :, None] * grad_wide[:, None, :]
    send_grads = jnp.einsum("tkj,tkd->jd", select, scaled, precision=lax.Precision.HIGHEST)
    grad_rows = spread(send_grads.astype(jnp.bfloat16).reshape(shape_slots))
    hidden_grad = jnp.einsum(
        "pqxcd,xfd->pqxcf", grad_rows, w_out, preferred_element_type=jnp.float32
    )
    pre_grad = (hidden_grad * gelu_slope(pre)).astype(jnp.bfloat16)
    w_out_grad = jnp.einsum(
        "pqxcf,pqxcd->xfd", hidden, grad_rows, preferred_element_type=jnp.float32
    )
    w_in_grad = jnp.einsum("pqxcd,pqxcf->xdf", rows, pre_grad, preferred_element_type=jnp.float32)

    def input_term(start, count):
        return jnp.einsum("pqxcf,xdf->pqxcd", pre_grad, w_in, preferred_element_type=jnp.float32)

    returned_grad = collect(input_term).reshape(columns, width)
    picked_grad = jnp.einsum(
        "tkj,jd->tkd", select_half, returned_grad, preferred_element_type=jnp.float32
    )
    tok_grad = jnp.sum(picked_grad, axis=1).astype(jnp.bfloat16)
    return (mixed, tok_grad, gate_grad, w_in_grad, w_out_grad)


def solution(mesh):
    placed = (
        P(("expert", "dp"), None),
        P(("expert", "dp"), None),
        P(("expert", "dp"), None),
        P(("expert", "dp"), None),
        P(("expert", "dp"), None),
        P("expert", None, "dp"),
        P("expert", "dp", None),
        P(("expert", "dp"), None),
    )
    return jax.shard_map(
        per_device,
        mesh=mesh,
        in_specs=placed,
        out_specs=(
            P(("expert", "dp"), None),
            P(("expert", "dp"), None),
            P(("expert", "dp"), None),
            P("expert", None, "dp"),
            P("expert", "dp", None),
        ),
        check_vma=False,
    )
```

profile of v0, /device:TPU:1, one launch (start us, length us, event | category | flops | bytes accessed | tf_op | source)
XLA Modules:
  0.0 618.3 jit_solution(17377462103736656560)
XLA Ops:
  7.2 0.8 broadcast_compare_fusion
  8.1 1.1 convert_element_type.61
  9.2 0.8 multiply_add_fusion
  10.1 1.5 fusion.14
  13.5 93.8 %all-gather.5.cloned.1.call-done = bf16[32,8,2,4,1664]{4,3,0,2,1:T(4,128)(2,1)} async-done(((bf16[1,8,2,4,1664]{4,3,0,2,1:T(4,128)(2,1)}), bf16[32,8,2,4,1664]{4,3,0,2,1:T(4,128)(2,1)}) %all-gather.5.cloned.1.call-update) | async-done | bytes 6815760 | tf_op jit(solution)/shard_map/all_gather | solution.py:25
  107.2 6.0 all-to-all-start.2
  113.3 85.9 %all-gather.3.cloned.1.call-done = bf16[32,8,2,4,1664]{4,3,0,2,1:T(4,128)(2,1)} async-done(((bf16[1,8,2,4,1664]{4,3,0,2,1:T(4,128)(2,1)}), bf16[32,8,2,4,1664]{4,3,0,2,1:T(4,128)(2,1)}) %all-gather.3.cloned.1.call-update) | async-done | bytes 6815760 | tf_op jit(solution)/shard_map/all_gather | solution.py:25
  199.2 6.0 all-to-all-start
  205.2 7.7 %fusion.4 = f32[2,32,8,4,256]{4,3,2,1,0:T(4,128)} fusion(bf16[32,8,2,4,1664]{4,3,0,2,1:T(4,128)(2,1)} %all-to-all-done.2, bf16[2,256,1664]{2,1,0:T(8,128)(2,1)S(1)} %copy-done.6), kind=kOutput, calls=%fused_computation.6 | convolution fusion | flops 1744830464 | bytes 10616832 | tf_op jit(solution)/shard_map/pqxcd,xfd->pqxcf/dot_general | solution.py:70
  212.9 69.3 %all-to-all-done = bf16[32,8,2,4,1664]{4,3,0,2,1:T(4,128)(2,1)} async-done(((bf16[32,8,2,4,1664]{4,3,0,2,1:T(4,128)(2,1)}), bf16[32,8,2,4,1664]{4,3,0,2,1:T(4,128)(2,1)}, u32[]{:S(2)}, u32[]{:S(2)}) %all-to-all-start) | async-done | bytes 6815776 | tf_op jit(solution)/shard_map/all_to_all | solution.py:26
  282.2 6.4 %fusion.6 = f32[2,32,8,4,256]{4,3,2,1,0:T(4,128)S(1)} fusion(bf16[32,8,2,4,1664]{4,3,0,2,1:T(4,128)(2,1)} %all-to-all-done, bf16[2,1664,256]{2,1,0:T(8,128)(2,1)S(1)} %copy-done), kind=kOutput, calls=%fused_computation.8 | convolution fusion | flops 1744830464 | bytes 10616832 | tf_op jit(solution)/shard_map/pqxcd,xdf->pqxcf/dot_general | solution.py:56
  288.7 1.4 fusion.20
  290.1 4.9 convert_bitcast_fusion
  295.0 4.9 convert_bitcast_fusion.1
  301.1 9.4 %fusion.8 = f32[2,256,1664]{2,1,0:T(8,128)} fusion(bf16[32,8,2,4,1664]{4,3,0,2,1:T(4,128)(2,1)} %all-to-all-done.2, bf16[32,8,2,4,256]{4,1,3,0,2:T(8,128)(2,1)S(1)} %copy-done.3), kind=kOutput, calls=%fused_computation.10 | convolution fusion | flops 1744830464 | bytes 11272192 | tf_op jit(solution)/shard_map/pqxcf,pqxcd->xfd/dot_general | solution.py:74
  310.6 265.1 %all-reduce.5.cloned.1.call-done = (bf16[32,8,2,4,1664]{4,1,3,0,2:T(8,128)(2,1)}, bf16[32,8,2,4,1664]{4,1,3,0,2:T(8,128)(2,1)}) async-done(((bf16[32,8,2,4,1664]{4,1,3,0,2:T(8,128)(2,1)}, bf16[32,8,2,4,1664]{4,1,3,0,2:T(8,128)(2,1)}), (bf16[32,8,2,4,1664]{4,1,3,0,2:T(8,128)(2,1)}, bf16[32,8,2,4,1664]{4,1,3,0,2:T(8,128)(2,1)})) %all-reduce.5.cloned.1.call-update) | async-done | bytes 13631504
  575.7 1.6 dynamic-slice_bitcast_fusion.1
  578.1 6.0 all-to-all-start.1
  584.0 1.6 dynamic-slice_bitcast_fusion
  586.4 3.7 all-to-all-done.1
  590.1 4.3 all-to-all-start.3
  594.4 13.5 %fusion.11 = f32[2,1664,256]{2,1,0:T(8,128)} fusion(bf16[32,8,2,4,1664]{4,3,0,2,1:T(4,128)(2,1)} %all-to-all-done, bf16[32,8,2,4,256]{4,1,3,0,2:T(8,128)(2,1)S(1)} %get-tuple-element.9), kind=kOutput, calls=%fused_computation.11 | convolution fusion | flops 1744830464 | bytes 11272192 | tf_op jit(solution)/shard_map/pqxcd,pqxcf->xdf/dot_general | solution.py:77
  607.9 2.6 multiply_reduce_fusion
  610.6 1.2 convolution_reduce_fusion
  (47 shorter events, 4.9 us)
Async XLA Ops:
  7.2 275.1 %copy-start = (bf16[2,1664,256]{2,1,0:T(8,128)(2,1)S(1)}, bf16[2,1664,256]{2,1,0:T(8,128)(2,1)}, u32[]{:S(2)}) copy-start(bf16[2,1664,256]{2,1,0:T(8,128)(2,1)} %param.13) | copy-start | bytes 5111812
  7.2 5.3 copy-start.8
  7.2 100.1 %all-gather.5.cloned.1.call-start = ((), (), s32[]{:S(2)}) async-start(), calls=%async_computation.5 | async-start | bytes 7028736 | tf_op jit(solution)/shard_map/all_gather | solution.py:25
  8.1 5.4 copy-start.11
  9.2 0.9 copy-start.4
  10.1 97.1 %copy-start.9 = (s32[128,2]{0,1:T(2,128)}, s32[128,2]{0,1:T(2,128)S(1)}, u32[]{:S(2)}) copy-start(s32[128,2]{0,1:T(2,128)S(1)} %multiply_add_fusion) | copy-start | bytes 3076
  12.4 186.8 %all-gather.3.cloned.1.call-start = ((), (), s32[]{:S(2)}) async-start(), calls=%async_computation.4 | async-start | bytes 7028736 | tf_op jit(solution)/shard_map/all_gather | solution.py:25
  107.2 92.0 %all-to-all-start.2 = ((bf16[32,8,2,4,1664]{4,3,0,2,1:T(4,128)(2,1)}), bf16[32,8,2,4,1664]{4,3,0,2,1:T(4,128)(2,1)}, u32[]{:S(2)}, u32[]{:S(2)}) async-start(bf16[32,8,2,4,1664]{4,3,0,2,1:T(4,128)(2,1)} %all-gather.5.cloned.1.call-done), calls=%async_computation.2 | async-start | bytes 13631488 | tf_op jit(solution)/shard_map/all_to_all | solution.py:26
  113.3 92.0 %copy-start.6 = (bf16[2,256,1664]{2,1,0:T(8,128)(2,1)S(1)}, bf16[2,256,1664]{2,1,0:T(8,128)(2,1)}, u32[]{:S(2)}) copy-start(bf16[2,256,1664]{2,1,0:T(8,128)(2,1)} %param.14) | copy-start | bytes 5111812
  199.2 83.0 %all-to-all-start = ((bf16[32,8,2,4,1664]{4,3,0,2,1:T(4,128)(2,1)}), bf16[32,8,2,4,1664]{4,3,0,2,1:T(4,128)(2,1)}, u32[]{:S(2)}, u32[]{:S(2)}) async-start(bf16[32,8,2,4,1664]{4,3,0,2,1:T(4,128)(2,1)} %all-gather.3.cloned.1.call-done), calls=%async_computation | async-start | bytes 13631488 | tf_op jit(solution)/shard_map/all_to_all | solution.py:26
  205.2 370.5 %all-reduce.5.cloned.1.call-start = ((), (), s32[]{:S(2)}) async-start(), calls=%async_computation.6 | async-start | bytes 27262976
  282.2 6.5 %copy-start.5 = (f32[2,32,8,4,256]{4,3,2,1,0:T(4,128)S(1)}, f32[2,32,8,4,256]{4,3,2,1,0:T(4,128)}, u32[]{:S(2)}) copy-start(f32[2,32,8,4,256]{4,3,2,1,0:T(4,128)} %fusion.4) | copy-start | bytes 6291460
  290.1 4.9 copy-start.2
  290.1 4.9 copy-start.7
  299.9 0.7 copy-start.14
  299.9 1.3 copy-start.3
  578.1 12.0 %all-to-all-start.1 = ((bf16[8,2,4,1664]{3,2,1,0:T(4,128)(2,1)}), bf16[8,2,4,1664]{3,2,1,0:T(4,128)(2,1)S(1)}, u32[]{:S(2)}, u32[]{:S(2)}) async-start(bf16[8,2,4,1664]{3,2,1,0:T(4,128)(2,1)} %copy.29), calls=%async_computation.1 | async-start | bytes 425984 | tf_op jit(solution)/shard_map/all_to_all | solution.py:36
  590.1 20.4 %all-to-all-start.3 = ((bf16[8,2,4,1664]{3,2,1,0:T(4,128)(2,1)}), bf16[8,2,4,1664]{3,2,1,0:T(4,128)(2,1)S(1)}, u32[]{:S(2)}, u32[]{:S(2)}) async-start(bf16[8,2,4,1664]{3,2,1,0:T(4,128)(2,1)} %copy.32), calls=%async_computation.3 | async-start | bytes 425984 | tf_op jit(solution)/shard_map/all_to_all | solution.py:36
  594.4 13.5 %copy-start.10 = (s32[128,2]{0,1:T(2,128)S(1)}, s32[128,2]{0,1:T(2,128)}, u32[]{:S(2)}) copy-start(s32[128,2]{0,1:T(2,128)} %copy-done.9) | copy-start | bytes 3076
  594.4 13.6 %copy-start.12 = (pred[128,2]{0,1:T(4,128)(4,1)S(1)}, pred[128,2]{0,1:T(4,128)(4,1)}, u32[]{:S(2)}) copy-start(pred[128,2]{0,1:T(4,128)(4,1)} %copy-done.11) | copy-start | bytes 772
  594.4 13.6 %copy-start.13 = (f32[128,2]{0,1:T(2,128)S(1)}, f32[128,2]{0,1:T(2,128)}, u32[]{:S(2)}) copy-start(f32[128,2]{0,1:T(2,128)} %param.12) | copy-start | bytes 3076
  594.4 17.4 %copy-start.1 = (bf16[2,1664,256]{2,1,0:T(8,128)(2,1)S(1)}, bf16[2,1664,256]{2,1,0:T(8,128)(2,1)}, u32[]{:S(2)}) copy-start(bf16[2,1664,256]{2,1,0:T(8,128)(2,1)} %param.13) | copy-start | bytes 5111812
Sparse Core Ops, SparseCore 0:
  12.5 94.6 all-gather.4
  110.4 88.7 all-gather.2
  300.0 275.6 all-reduce.4
where the time goes:
time: 619 us; the launch traced here: 618 us
  waiting for transfers between devices  518 us (84%)
  matrix products  52.2 us (8%)
  starting transfers between devices  22.3 us (4%)
  between operations  13.9 us (2%)
  local copies, waits for them, and re-layouts  7.77 us (1%)
    unnamed x4, waiting for transfers between devices  265 us
    all_gather x2, waiting for transfers between devices, spread(): grouped = lax.all_gather(buffer[None], 'dp', axis=0, tiled=True)  180 us
    all_to_all x2, waiting for transfers between devices, spread(): lax.all_to_all(grouped, 'expert', split_axis=1, concat_axis=1, tiled=True)  69.3 us
    dot_general x1, matrix products, per_device(): jnp.einsum('pqxcd,pqxcf->xdf', rows, pre_grad, preferred_element_type=jnp...  13.5 us
  transfers between devices with their start and end apart: 7, of which 5 were waited for; matrix products, arithmetic and copies ran while one was open for 6% of the time, Pallas kernels for 0%

commit v1 on v0

v1 whole, which is shorter than its diff:
```python
import jax
import jax.numpy as jnp
from jax import lax
from jax.experimental import pallas as pl
from jax.experimental.pallas import tpu as pltpu
from jax.sharding import PartitionSpec as P

CAP = 4
N_EXP = 8
N_DP = 32
HALF = 16
BF16 = jnp.bfloat16
F32 = jnp.float32
MESH = pl.DeviceIdType.MESH

inv_root_two = 0.7071067811865476
inv_root_two_pi = 0.3989422804014327


def place_first(y, z):
    return 4 * z + (y + z) % 4


def device_first(p):
    z = p // 4
    return ((p % 4 + 8 - z) % 4) * 8 + z


def place_second(y, z):
    w = (z + 24 - 3 * y) % 8
    return 4 * y + 16 * (w // 4) + w % 4


def device_second(p):
    q = p // 4
    return (q % 4) * 8 + (3 * q + p % 4) % 8


def dot(left, right, left_dim, right_dim):
    return lax.dot_general(
        left, right, (((left_dim,), (right_dim,)), ((), ())), preferred_element_type=F32
    )


def kernel(
    tokens, ids, slots, dropped, gates, out_grad, w_in_hbm, w_out_hbm,
    mixed, tok_grad, gate_grad, w_in_grad, w_out_grad,
    gathered, part, arrived, hidden, pre_grad, w_in, w_out, send, recv, back,
    load_sem, a2a_send, a2a_recv, ag_send, ag_recv, rs_send, rs_recv, ret_send, ret_recv,
):
    width = tokens.shape[1]
    me_e = lax.axis_index("expert")
    me_d = lax.axis_index("dp")
    y, z = me_d // 8, me_d % 8
    here = (place_first(y, z), place_second(y, z))
    device = (device_first, device_second)
    near = [[device[c]((here[c] + step) % N_DP) for step in (1, N_DP - 1)] for c in range(2)]

    load_in = pltpu.make_async_copy(w_in_hbm, w_in, load_sem.at[0])
    load_out = pltpu.make_async_copy(w_out_hbm, w_out, load_sem.at[1])
    load_in.start()
    load_out.start()

    barrier = pltpu.get_barrier_semaphore()

    def greet(k, carry):
        pl.semaphore_signal(
            barrier, inc=1, device_id={"expert": (me_e + k) % N_EXP}, device_id_type=MESH
        )
        return carry

    lax.fori_loop(1, N_EXP, greet, 0)
    for c in range(2):
        for d in range(2):
            pl.semaphore_signal(barrier, inc=1, device_id={"dp": near[c][d]}, device_id_type=MESH)

    expert = ids[...]
    column = (expert >> 1) * 16 + (expert & 1) * 4 + slots[...]
    column = jnp.where(dropped[...] == 0, column, -64)
    lane = lax.broadcasted_iota(jnp.int32, (128, 128), 1)
    pick = [column[:, k : k + 1] == lane for k in range(2)]
    pick_grad = [column[:, k : k + 1] + 8 == lane for k in range(2)]

    def onehot(mask):
        return jnp.where(mask, 1.0, 0.0).astype(BF16)

    grad_wide = out_grad[...].astype(F32)
    packed = dot(onehot(pick[0] | pick[1]), tokens[...], 0, 0)
    for k in range(2):
        scaled = (gates[:, k : k + 1] * grad_wide).astype(BF16)
        packed += dot(onehot(pick_grad[k]), scaled, 0, 0)
    send[...] = packed.astype(BF16).reshape(N_EXP, 16, width)
    pl.semaphore_wait(barrier, N_EXP + 3)

    def across(source, target, k, sems):
        return pltpu.make_async_remote_copy(
            src_ref=source.at[(me_e + k) % N_EXP],
            dst_ref=target.at[me_e],
            send_sem=sems[0].at[k],
            recv_sem=sems[1].at[k],
            device_id={"expert": (me_e + k) % N_EXP},
            device_id_type=MESH,
        )

    def exchange(source, target, sems):
        own = pltpu.make_async_copy(source.at[me_e], target.at[me_e], sems[0].at[0])
        own.start()

        def go(k, carry):
            across(source, target, k, sems).start()
            return carry

        def done(k, carry):
            across(source, target, k, sems).wait()
            return carry

        lax.fori_loop(1, N_EXP, go, 0)
        own.wait()
        lax.fori_loop(1, N_EXP, done, 0)

    exchange(send, recv, (a2a_send, a2a_recv))

    row = lax.broadcasted_iota(jnp.int32, (128, 128), 0)
    source_row = ((row & 31) >> 2) * 16 + ((row >> 5) & 1) * 8 + (row >> 6) * 4 + (row & 3)
    shuffle = onehot(source_row == lane)
    block = dot(shuffle, recv[...].reshape(128, width), 1, 0).astype(BF16)
    for c in range(2):
        for a in range(2):
            gathered[c, a, HALF] = block[(c * 2 + a) * 32 : (c * 2 + a + 1) * 32]

    def gather_copy(c, d, a, s):
        return pltpu.make_async_remote_copy(
            src_ref=gathered.at[c, a, HALF + 1 - s if d == 0 else HALF - 1 + s],
            dst_ref=gathered.at[c, a, HALF - s if d == 0 else (HALF + s) % N_DP],
            send_sem=ag_send.at[c, d, a, s - 1],
            recv_sem=ag_recv.at[c, d, a, s - 1],
            device_id={"dp": near[c][d]},
            device_id_type=MESH,
        )

    def experts(c, rows, grads):
        count = rows.shape[0]
        pre = dot(rows, w_in[c], 1, 0)
        erf = 1.0 + lax.erf(pre * inv_root_two)
        hid = (0.5 * pre * erf).astype(BF16)
        slope = 0.5 * erf + pre * jnp.exp(-0.5 * pre * pre) * inv_root_two_pi
        grad = (dot(grads, w_out[c], 1, 1) * slope).astype(BF16)
        out = dot(hid, w_out[c], 1, 0).astype(BF16)
        row_grad = dot(grad, w_in[c], 1, 1).astype(BF16)
        shape = (count // 32, 32, -1)
        return [v.reshape(shape) for v in (hid, grad, out, row_grad)]

    def keep(c, at, values, first):
        hid, grad, out, row_grad = (v[first : first + at.size] for v in values)
        hidden[c, at] = hid
        pre_grad[c, at] = grad
        part[c, 0, at] = out
        part[c, 1, at] = row_grad

    def gather_step(s, carry):
        @pl.when(s <= HALF)
        def _():
            for a in range(2):
                for c in range(2):
                    for d in range(2):
                        @pl.when(s > 1)
                        def _():
                            gather_copy(c, d, a, s - 1).wait_recv()

                        if d == a:
                            gather_copy(c, d, a, s).start()
                        else:
                            @pl.when(s < HALF)
                            def _():
                                gather_copy(c, d, a, s).start()

        @pl.when(s == 2)
        def _():
            load_in.wait()
            load_out.wait()

        @pl.when(s > 1)
        def _():
            c = s % 2
            base = s - 2 - c
            behind, ahead = pl.ds(HALF - 1 - base, 2), pl.ds(HALF + base, 2)

            def both(a):
                return jnp.concatenate(
                    [gathered[c, a, behind].reshape(64, width), gathered[c, a, ahead].reshape(64, width)]
                )

            values = experts(c, both(0), both(1))
            keep(c, behind, values, 0)
            keep(c, ahead, values, 2)

        return carry

    lax.fori_loop(1, HALF + 2, gather_step, 0)
    for c in range(2):
        for a in range(2):
            gather_copy(c, a, a, HALF).wait_recv()
        keep(c, pl.ds(0, 1), experts(c, gathered[c, 0, 0], gathered[c, 1, 0]), 0)

    def sum_slot(d, t):
        return (N_DP + 1 - t) % N_DP if d == 0 else t - 1

    def sum_copy(c, d, a, t):
        return pltpu.make_async_remote_copy(
            src_ref=part.at[c, a, sum_slot(d, t)],
            dst_ref=arrived.at[c, a, N_DP - t if d == 0 else t % HALF],
            send_sem=rs_send.at[c, d, a, t - 1],
            recv_sem=rs_recv.at[c, d, a, t - 1],
            device_id={"dp": near[c][d]},
            device_id_type=MESH,
        )

    def sum_step(t, carry):
        for a in range(2):
            for c in range(2):
                for d in range(2):
                    first = 1 if d == a else 2

                    @pl.when(t > first)
                    def _():
                        sum_copy(c, d, a, t - 1).wait_recv()
                        slot = sum_slot(d, t)
                        part[c, a, slot] = (
                            part[c, a, slot].astype(F32) + arrived[c, a, slot].astype(F32)
                        ).astype(BF16)

                    @pl.when(t >= first)
                    def _():
                        sum_copy(c, d, a, t).start()

        @pl.when(t <= width // 128)
        def _():
            cut = pl.ds(pl.multiple_of((t - 1) * 128, 128), 128)
            for c in range(2):
                w_in_grad[c, cut, :] = dot(
                    gathered[c, 0, :, :, cut].reshape(1024, 128), pre_grad[c].reshape(1024, -1), 0, 0
                )
                w_out_grad[c, :, cut] = dot(
                    hidden[c].reshape(1024, -1), gathered[c, 1, :, :, cut].reshape(1024, 128), 0, 0
                )

        return carry

    lax.fori_loop(1, HALF + 1, sum_step, 0)
    total = []
    for c in range(2):
        for a in range(2):
            for d in range(2):
                sum_copy(c, d, a, HALF).wait_recv()
            total.append(
                (
                    part[c, a, HALF].astype(F32)
                    + arrived[c, a, HALF].astype(F32)
                    + arrived[c, a, 0].astype(F32)
                ).astype(BF16)
            )
    send[...] = dot(shuffle, jnp.concatenate(total), 0, 0).astype(BF16).reshape(N_EXP, 16, width)
    exchange(send, back, (ret_send, ret_recv))

    returned = back[...].reshape(128, width)
    picked = [dot(onehot(pick[k]), returned, 1, 0) for k in range(2)]
    mixed[...] = (gates[:, 0:1] * picked[0] + gates[:, 1:2] * picked[1]).astype(BF16)
    gate_grad[...] = jnp.concatenate(
        [jnp.sum(picked[k] * grad_wide, axis=1, keepdims=True) for k in range(2)], axis=1
    )
    tok_grad[...] = dot(onehot(pick_grad[0] | pick_grad[1]), returned, 1, 0).astype(BF16)

    def drain(s, carry):
        for c in range(2):
            for d in range(2):
                for a in range(2):
                    if d == a:
                        gather_copy(c, d, a, s).wait_send()
                        sum_copy(c, d, a, s).wait_send()
                    else:
                        @pl.when(s < HALF)
                        def _():
                            gather_copy(c, d, a, s).wait_send()
                            sum_copy(c, d, a, s + 1).wait_send()
        return carry

    lax.fori_loop(1, HALF + 1, drain, 0)


def per_device(tokens, expert_ids, slot_ids, dropped, gates, w_in, w_out, out_grad):
    count, width = tokens.shape
    hidden_units = w_in.shape[2]
    vmem = pl.BlockSpec(memory_space=pltpu.VMEM)
    anywhere = pl.BlockSpec(memory_space=pl.ANY)
    blocks = pltpu.VMEM((2, 2, N_DP, 32, width), BF16)
    units = pltpu.VMEM((2, N_DP, 32, hidden_units), BF16)
    small = pltpu.VMEM((N_EXP, 16, width), BF16)
    dma = pltpu.SemaphoreType.DMA
    return pl.pallas_call(
        kernel,
        out_shape=(
            jax.ShapeDtypeStruct((count, width), BF16),
            jax.ShapeDtypeStruct((count, width), BF16),
            jax.ShapeDtypeStruct((count, 2), F32),
            jax.ShapeDtypeStruct(w_in.shape, F32),
            jax.ShapeDtypeStruct(w_out.shape, F32),
        ),
        in_specs=[vmem] * 6 + [anywhere] * 2,
        out_specs=[vmem] * 5,
        scratch_shapes=[
            blocks, blocks, blocks, units, units,
            pltpu.VMEM(w_in.shape, BF16), pltpu.VMEM(w_out.shape, BF16),
            small, small, small,
            dma((2,)), dma((N_EXP,)), dma((N_EXP,)),
            dma((2, 2, 2, HALF)), dma((2, 2, 2, HALF)), dma((2, 2, 2, HALF)), dma((2, 2, 2, HALF)),
            dma((N_EXP,)), dma((N_EXP,)),
        ],
        compiler_params=pltpu.CompilerParams(
            collective_id=0, has_side_effects=True, vmem_limit_bytes=60 * 1024 * 1024
        ),
        cost_estimate=pl.CostEstimate(
            flops=12 * 2048 * width * hidden_units, bytes_accessed=20_000_000, transcendentals=2_000_000
        ),
    )(tokens, expert_ids, slot_ids, dropped, gates, out_grad, w_in, w_out)


def solution(mesh):
    rows = P(("expert", "dp"), None)
    placed = (rows, rows, rows, rows, rows, P("expert", None, "dp"), P("expert", "dp", None), rows)
    return jax.shard_map(
        per_device,
        mesh=mesh,
        in_specs=placed,
        out_specs=(rows, rows, rows, P("expert", None, "dp"), P("expert", "dp", None)),
        check_vma=False,
    )
```

time: 619 us -> 211 us (0.34)
  waiting for transfers between devices: 518 us -> 0 us
  Pallas kernels: 0 us -> 194 us
  matrix products: 52.2 us -> 0 us
  starting transfers between devices: 22.3 us -> 0 us
  between operations: 13.9 us -> 0.64 us
  local copies, waits for them, and re-layouts: 7.77 us -> 16.6 us
    unnamed x4 -> x0, waiting for transfers between devices: 265 us -> none
    pallas_call x0 -> x1, Pallas kernels: none -> 194 us  [per_device(): pl.pallas_call(kernel, out_shape=(jax.ShapeDtypeStruct((count, width), BF...]
    all_gather x2 -> x0, waiting for transfers between devices: 180 us -> none  [spread(): grouped = lax.all_gather(buffer[None], 'dp', axis=0, tiled=True)]
    all_to_all x4 -> x0, waiting for transfers between devices: 73 us -> none  [the longest x2 69.3 us: spread(): lax.all_to_all(grouped, 'expert', split_axis=1, concat_axis=1, tiled=True)]
    dot_general x10 -> x0, matrix products: 52.2 us -> none  [the longest x1 13.5 us: per_device(): jnp.einsum('pqxcd,pqxcf->xdf', rows, pre_grad, preferred_element_type=jnp...]
    all_to_all x4 -> x0, starting transfers between devices: 22.3 us -> none  [the longest x2 12 us: spread(): lax.all_to_all(grouped, 'expert', split_axis=1, concat_axis=1, tiled=True)]
    unnamed x31 -> x10, local copies, waits for them, and re-layouts: 1.46 us -> 15.1 us
  transfers between devices with their start and end apart: 7 -> 0, of which waited for: 5 -> 0; matrix products, arithmetic and copies ran while one was open for 6% -> 0% of each run, Pallas kernels for 0% -> 0%
where the time goes in v1:
time: 211 us
  Pallas kernels  194 us (92%)
  local copies, waits for them, and re-layouts  16.6 us (8%)
    pallas_call x1, Pallas kernels, per_device(): pl.pallas_call(kernel, out_shape=(jax.ShapeDtypeStruct((count, width), BF...  194 us
    unnamed x10, local copies, waits for them, and re-layouts  15.1 us

profile of v1, /device:TPU:1, one launch (start us, length us, event | category | flops | bytes accessed | tf_op | source)
XLA Modules:
  0.0 210.8 jit_solution(791053923517584702)
XLA Ops:
  0.6 1.4 copy.13.ids
  2.0 1.4 copy.14.slots
  3.5 1.4 copy.15.dropped
  4.9 1.4 copy.16.gates
  6.3 193.6 %shard_map.119 = (bf16[128,1664]{1,0:T(8,128)(2,1)}, bf16[128,1664]{1,0:T(8,128)(2,1)}, f32[128,2]{1,0:T(8,128)}, f32[2,1664,256]{2,1,0:T(8,128)}, f32[2,256,1664]{2,1,0:T(8,128)}) custom-call(bf16[128,1664]{1,0:T(8,128)(2,1)} %tokens.1, s32[128,2]{1,0:T(8,128)} %copy.13.ids, s32[128,2]{1,0:T(8,128)} %copy.14.slots, s32[128,2]{1,0:T(8,128)} %copy.15.dropped, ...), custom_call_target="tpu_custom_call" | custom-call | flops 10468982784 | bytes 20000000 | tf_op jit(solution)/shard_map/pallas_call | solution.py:299
  199.9 1.5 copy.17
  201.3 1.8 copy.22
  203.1 1.8 copy.23
  204.9 0.0 copy-start
  204.9 4.1 %copy.24 = f32[2,1664,256]{2,1,0:T(8,128)} copy(f32[2,1664,256]{2,1,0:T(8,128)} %get-tuple-element.18) | data formatting | bytes 6815744
  209.0 0.0 copy-done
  209.0 1.8 copy.25
Async XLA Ops:
  204.9 4.1 %copy-start = (f32[2,256,1664]{2,1,0:T(8,128)S(1)}, f32[2,256,1664]{2,1,0:T(8,128)}, u32[]{:S(2)}) copy-start(f32[2,256,1664]{2,1,0:T(8,128)} %get-tuple-element.19) | copy-start | bytes 10223620

commit v2 on v1

v2 whole, which is shorter than its diff:
```python
import jax
import jax.numpy as jnp
from jax import lax
from jax.experimental import pallas as pl
from jax.experimental.pallas import tpu as pltpu
from jax.sharding import PartitionSpec as P

CAP = 4
N_EXP = 8
N_DP = 32
HALF = 16
BF16 = jnp.bfloat16
F32 = jnp.float32
MESH = pl.DeviceIdType.MESH

inv_root_two = 0.7071067811865476
inv_root_two_pi = 0.3989422804014327


def place_first(y, z):
    return 4 * z + (y + z) % 4


def device_first(p):
    z = p // 4
    return ((p % 4 + 8 - z) % 4) * 8 + z


def place_second(y, z):
    w = (z + 24 - 3 * y) % 8
    return 4 * y + 16 * (w // 4) + w % 4


def device_second(p):
    q = p // 4
    return (q % 4) * 8 + (3 * q + p % 4) % 8


def dot(left, right, left_dim, right_dim):
    return lax.dot_general(
        left, right, (((left_dim,), (right_dim,)), ((), ())), preferred_element_type=F32
    )


def kernel(
    tokens, ids, slots, dropped, gates, out_grad, w_in_hbm, w_out_hbm,
    mixed, tok_grad, gate_grad, w_in_grad, w_out_grad,
    gathered, part, arrived, hidden, pre_grad, w_in, w_out, send, recv, back,
    load_sem, a2a_send, a2a_recv, ag_send, ag_recv, rs_send, rs_recv, ret_send, ret_recv,
):
    width = tokens.shape[1]
    left = send.shape[3]
    me_e = lax.axis_index("expert")
    me_d = lax.axis_index("dp")
    y, z = me_d // 8, me_d % 8
    here = (place_first(y, z), place_second(y, z))
    device = (device_first, device_second)
    near = [[device[c]((here[c] + step) % N_DP) for step in (1, N_DP - 1)] for c in range(2)]

    def beside(c, d):
        return {"dp": near[0][d] + c * (near[1][d] - near[0][d])}

    load_in = pltpu.make_async_copy(w_in_hbm, w_in, load_sem.at[0])
    load_out = pltpu.make_async_copy(w_out_hbm, w_out, load_sem.at[1])
    load_in.start()
    load_out.start()

    barrier = pltpu.get_barrier_semaphore()

    def greet(k, carry):
        pl.semaphore_signal(
            barrier, inc=1, device_id={"expert": (me_e + k) % N_EXP}, device_id_type=MESH
        )
        return carry

    lax.fori_loop(1, N_EXP, greet, 0)
    for c in range(2):
        for d in range(2):
            pl.semaphore_signal(barrier, inc=1, device_id={"dp": near[c][d]}, device_id_type=MESH)

    expert = ids[...]
    column = (expert >> 1) * 16 + (expert & 1) * 4 + slots[...]
    column = jnp.where(dropped[...] == 0, column, -64)
    row = lax.broadcasted_iota(jnp.int32, (128, 128), 0)
    lane = lax.broadcasted_iota(jnp.int32, (128, 128), 1)

    def onehot(mask):
        return jnp.where(mask, 1.0, 0.0).astype(BF16)

    chosen = [[onehot(column[k : k + 1, :] + 8 * h == row) for h in range(2)] for k in range(2)]
    gate = [jnp.broadcast_to(gates[k : k + 1, :], (128, 128)).T[:, :1] for k in range(2)]
    pad = 2 * left - width

    def halves(value):
        zeros = jnp.zeros((value.shape[0], pad), BF16)
        return value[:, :left], jnp.concatenate([value[:, left:], zeros], axis=1)

    def pack(a, values):
        packed = sum(dot(chosen[k][h], values[k][h], 1, 0) for k in range(2) for h in range(2))
        send[a] = packed.astype(BF16).reshape(N_EXP, 16, left)

    def across(source, target, a, k, sems):
        return pltpu.make_async_remote_copy(
            src_ref=source.at[a, (me_e + k) % N_EXP],
            dst_ref=target.at[a, me_e],
            send_sem=sems[0].at[a, k],
            recv_sem=sems[1].at[a, k],
            device_id={"expert": (me_e + k) % N_EXP},
            device_id_type=MESH,
        )

    def exchange_start(source, target, a, sems):
        def go(k, carry):
            across(source, target, a, k, sems).start()
            return carry

        lax.fori_loop(1, N_EXP, go, 0)
        target[a, me_e] = source[a, me_e]

    def exchange_wait(source, target, a, sems):
        def done(k, carry):
            across(source, target, a, k, sems).wait()
            return carry

        lax.fori_loop(1, N_EXP, done, 0)

    out_way = (a2a_send, a2a_recv)
    token_halves = halves(tokens[...])
    pack(0, (token_halves, token_halves))
    pl.semaphore_wait(barrier, N_EXP + 3)
    exchange_start(send, recv, 0, out_way)
    pack(1, [halves((gate[k] * out_grad[...].astype(F32)).astype(BF16)) for k in range(2)])
    exchange_start(send, recv, 1, out_way)

    out_row = row[:64]
    source_row = ((out_row & 31) >> 2) * 16 + (out_row >> 5) * 4 + (out_row & 3)
    shuffle = [onehot(source_row + 8 * h == lane[:64]) for h in range(2)]

    def gather_copy(c, d, a, s):
        return pltpu.make_async_remote_copy(
            src_ref=gathered.at[c, a, HALF + 1 - s if d == 0 else HALF - 1 + s],
            dst_ref=gathered.at[c, a, HALF - s if d == 0 else (HALF + s) % N_DP],
            send_sem=ag_send.at[c, d, a, s - 1],
            recv_sem=ag_recv.at[c, d, a, s - 1],
            device_id=beside(c, d),
            device_id_type=MESH,
        )

    for a in range(2):
        exchange_wait(send, recv, a, out_way)
        got = recv[a].reshape(128, left)
        for h in range(2):
            block = dot(shuffle[h], got, 1, 0).astype(BF16)
            for c in range(2):
                if h == 0:
                    gathered[c, a, HALF, :, :left] = block[c * 32 : (c + 1) * 32]
                else:
                    gathered[c, a, HALF, :, left:] = block[c * 32 : (c + 1) * 32, : width - left]
        for c in range(2):
            for d in range(2):
                gather_copy(c, d, a, 1).start()

    def experts(c, rows, grads):
        count = rows.shape[0]
        pre = dot(rows, w_in[c], 1, 0)
        erf = 1.0 + lax.erf(pre * inv_root_two)
        hid = (0.5 * pre * erf).astype(BF16)
        slope = 0.5 * erf + pre * jnp.exp(-0.5 * pre * pre) * inv_root_two_pi
        grad = (dot(grads, w_out[c], 1, 1) * slope).astype(BF16)
        out = dot(hid, w_out[c], 1, 0).astype(BF16)
        row_grad = dot(grad, w_in[c], 1, 1).astype(BF16)
        shape = (count // 32, 32, -1)
        return [v.reshape(shape) for v in (hid, grad, out, row_grad)]

    def keep(c, at, values, first):
        hid, grad, out, row_grad = (v[first : first + at.size] for v in values)
        hidden[c, at] = hid
        pre_grad[c, at] = grad
        part[c, 0, at] = out
        part[c, 1, at] = row_grad

    def sum_slot(d, t):
        return (N_DP + 1 - t) % N_DP if d == 0 else t - 1

    def sum_copy(c, d, a, t):
        return pltpu.make_async_remote_copy(
            src_ref=part.at[c, a, sum_slot(d, t)],
            dst_ref=arrived.at[c, a, N_DP - t if d == 0 else t % HALF],
            send_sem=rs_send.at[c, d, a, t - 1],
            recv_sem=rs_recv.at[c, d, a, t - 1],
            device_id=beside(c, d),
            device_id_type=MESH,
        )

    def gather_step(s, carry):
        @pl.when(s <= HALF)
        def _():
            for a in range(2):
                for c in range(2):
                    for d in range(2):
                        gather_copy(c, d, a, s - 1).wait_recv()
                        if d == a:
                            gather_copy(c, d, a, s).start()
                        else:
                            @pl.when(s < HALF)
                            def _():
                                gather_copy(c, d, a, s).start()

        @pl.when(s == 2)
        def _():
            load_in.wait()
            load_out.wait()

        c = s % 2
        base = s - 2 - c
        behind, ahead = pl.ds(HALF - 1 - base, 2), pl.ds(HALF + base, 2)

        def both(a):
            return jnp.concatenate(
                [gathered[c, a, behind].reshape(64, width), gathered[c, a, ahead].reshape(64, width)]
            )

        values = experts(c, both(0), both(1))
        keep(c, behind, values, 0)
        keep(c, ahead, values, 2)

        @pl.when(s >= HALF)
        def _():
            for a in range(2):
                sum_copy(c, 1 - a, a, 2).start()

        return carry

    lax.fori_loop(2, HALF + 2, gather_step, 0)
    for c in range(2):
        for a in range(2):
            gather_copy(c, a, a, HALF).wait_recv()
        keep(c, pl.ds(0, 1), experts(c, gathered[c, 0, 0], gathered[c, 1, 0]), 0)
        for a in range(2):
            sum_copy(c, a, a, 1).start()

    def add(c, d, a, t):
        sum_copy(c, d, a, t - 1).wait_recv()
        slot = sum_slot(d, t)
        part[c, a, slot] = (part[c, a, slot].astype(F32) + arrived[c, a, slot].astype(F32)).astype(BF16)
        sum_copy(c, d, a, t).start()

    def sum_step(t, carry):
        for c in range(2):
            for a in range(2):
                @pl.when(t < HALF)
                def _():
                    add(c, 1 - a, a, t + 1)

        for c in range(2):
            for a in range(2):
                add(c, a, a, t)

        @pl.when(t <= width // 128 + 1)
        def _():
            cut = pl.ds(pl.multiple_of((t - 2) * 128, 128), 128)
            for c in range(2):
                w_in_grad[c, cut, :] = dot(
                    gathered[c, 0, :, :, cut].reshape(1024, 128), pre_grad[c].reshape(1024, -1), 0, 0
                )
                w_out_grad[c, :, cut] = dot(
                    hidden[c].reshape(1024, -1), gathered[c, 1, :, :, cut].reshape(1024, 128), 0, 0
                )

        return carry

    lax.fori_loop(2, HALF + 1, sum_step, 0)
    home = (ret_send, ret_recv)
    for a in range(2):
        total = []
        for c in range(2):
            for d in range(2):
                sum_copy(c, d, a, HALF).wait_recv()
            total.append(
                (
                    part[c, a, HALF].astype(F32)
                    + arrived[c, a, HALF].astype(F32)
                    + arrived[c, a, 0].astype(F32)
                ).astype(BF16)
            )
        total = halves(jnp.concatenate(total))
        packed = sum(dot(shuffle[h], total[h], 0, 0) for h in range(2))
        send[a] = packed.astype(BF16).reshape(N_EXP, 16, left)
        exchange_start(send, back, a, home)

    def drain(s, carry):
        for c in range(2):
            for d in range(2):
                for a in range(2):
                    if d == a:
                        gather_copy(c, d, a, s).wait_send()
                        sum_copy(c, d, a, s).wait_send()
                    else:
                        @pl.when(s < HALF)
                        def _():
                            gather_copy(c, d, a, s).wait_send()
                            sum_copy(c, d, a, s + 1).wait_send()
        return carry

    lax.fori_loop(1, HALF + 1, drain, 0)

    def unpack(a, k):
        returned = back[a].reshape(128, left)
        first, second = (dot(chosen[k][h], returned, 0, 0) for h in range(2))
        return jnp.concatenate([first, second[:, : width - left]], axis=1)

    exchange_wait(send, back, 0, home)
    grad_wide = out_grad[...].astype(F32)
    picked = [unpack(0, k) for k in range(2)]
    mixed[...] = (gate[0] * picked[0] + gate[1] * picked[1]).astype(BF16)
    for k in range(2):
        inner = jnp.sum(picked[k] * grad_wide, axis=1, keepdims=True)
        gate_grad[k : k + 1, :] = jnp.broadcast_to(inner, (128, 128)).T[:1]
    exchange_wait(send, back, 1, home)
    tok_grad[...] = (unpack(1, 0) + unpack(1, 1)).astype(BF16)


def per_device(tokens, expert_ids, slot_ids, dropped, gates, w_in, w_out, out_grad):
    count, width = tokens.shape
    hidden_units = w_in.shape[2]
    vmem = pl.BlockSpec(memory_space=pltpu.VMEM)
    anywhere = pl.BlockSpec(memory_space=pl.ANY)
    blocks = pltpu.VMEM((2, 2, N_DP, 32, width), BF16)
    units = pltpu.VMEM((2, N_DP, 32, hidden_units), BF16)
    small = pltpu.VMEM((2, N_EXP, 16, (width // 128 + 1) // 2 * 128), BF16)
    dma = pltpu.SemaphoreType.DMA
    mixed, tok_grad, gate_grad, w_in_grad, w_out_grad = pl.pallas_call(
        kernel,
        out_shape=(
            pltpu.VMEM((count, width), BF16),
            pltpu.VMEM((count, width), BF16),
            pltpu.VMEM((2, count), F32),
            pltpu.VMEM(w_in.shape, F32),
            pltpu.VMEM(w_out.shape, F32),
        ),
        in_specs=[vmem] * 6 + [anywhere] * 2,
        scratch_shapes=[
            blocks, blocks, blocks, units, units,
            pltpu.VMEM(w_in.shape, BF16), pltpu.VMEM(w_out.shape, BF16),
            small, small, small,
            dma((2,)), dma((2, N_EXP)), dma((2, N_EXP)),
            dma((2, 2, 2, HALF)), dma((2, 2, 2, HALF)), dma((2, 2, 2, HALF)), dma((2, 2, 2, HALF)),
            dma((2, N_EXP)), dma((2, N_EXP)),
        ],
        compiler_params=pltpu.CompilerParams(
            collective_id=0, has_side_effects=True, vmem_limit_bytes=50 * 1024 * 1024
        ),
        cost_estimate=pl.CostEstimate(
            flops=12 * 2048 * width * hidden_units, bytes_accessed=20_000_000, transcendentals=2_000_000
        ),
    )(tokens, expert_ids.T, slot_ids.T, dropped.T, gates.T, out_grad, w_in, w_out)
    return mixed, tok_grad, gate_grad.T, w_in_grad, w_out_grad


def solution(mesh):
    rows = P(("expert", "dp"), None)
    placed = (rows, rows, rows, rows, rows, P("expert", None, "dp"), P("expert", "dp", None), rows)
    return jax.shard_map(
        per_device,
        mesh=mesh,
        in_specs=placed,
        out_specs=(rows, rows, rows, P("expert", None, "dp"), P("expert", "dp", None)),
        check_vma=False,
    )
```

time: 211 us -> 193 us (0.915)
  local copies, waits for them, and re-layouts: 16.6 us -> 5.58 us
  Pallas kernels: 194 us -> 186 us
    unnamed x10 -> x5, local copies, waits for them, and re-layouts: 15.1 us -> 5.58 us
    pallas_call x1, Pallas kernels: 194 us -> 186 us  [per_device(): pl.pallas_call(kernel, out_shape=(pltpu.VMEM((count, width), BF16), pltpu...]
where the time goes in v2:
time: 193 us
  Pallas kernels  186 us (96%)
  local copies, waits for them, and re-layouts  5.58 us (3%)
    pallas_call x1, Pallas kernels, per_device(): pl.pallas_call(kernel, out_shape=(pltpu.VMEM((count, width), BF16), pltpu...  186 us
    unnamed x5, local copies, waits for them, and re-layouts  5.58 us

profile of v2, /device:TPU:1, one launch (start us, length us, event | category | flops | bytes accessed | tf_op | source)
XLA Modules:
  0.0 192.7 jit_solution(5502669415773062722)
XLA Ops:
  0.6 186.5 %shard_map.119 = (bf16[128,1664]{1,0:T(8,128)(2,1)S(1)}, bf16[128,1664]{1,0:T(8,128)(2,1)S(1)}, f32[2,128]{1,0:T(2,128)S(1)}, f32[2,1664,256]{2,1,0:T(8,128)S(1)}, f32[2,256,1664]{2,1,0:T(8,128)S(1)}) custom-call(bf16[128,1664]{1,0:T(8,128)(2,1)} %tokens.1, s32[2,128]{1,0:T(2,128)} %bitcast.6, s32[2,128]{1,0:T(2,128)} %bitcast.7, s32[2,128]{1,0:T(2,128)} %bitcast.8, ...), custom_call_target="tpu_custom_call" | custom-call | flops 10468982784 | bytes 20000000 | tf_op jit(solution)/shard_map/pallas_call | solution.py:332
  187.1 0.8 copy.18
  187.9 0.6 copy.20
  188.4 0.8 copy.19
  189.2 1.7 copy.21
  190.9 1.7 copy.22

commit v3 on v2

--- a/solution.py
+++ b/solution.py
@@ -12,6 +12,7 @@
 BF16 = jnp.bfloat16
 F32 = jnp.float32
 MESH = pl.DeviceIdType.MESH
+ORDER = [(a, h, c, d) for a in range(2) for h in range(2) for c in range(2) for d in range(2)]
 
 inv_root_two = 0.7071067811865476
 inv_root_two_pi = 0.3989422804014327
@@ -43,9 +44,10 @@
 
 
 def kernel(
-    tokens, ids, slots, dropped, gates, out_grad, w_in_hbm, w_out_hbm,
+    tokens_in, ids_in, slots_in, dropped_in, gates_in, out_grad_in, w_in_in, w_out_in,
     mixed, tok_grad, gate_grad, w_in_grad, w_out_grad,
-    gathered, part, arrived, hidden, pre_grad, w_in, w_out, send, recv, back,
+    tokens, ids, slots, dropped, gates, out_grad, w_in, w_out,
+    gathered, part, arrived, hidden, pre_grad, send, recv, back,
     load_sem, a2a_send, a2a_recv, ag_send, ag_recv, rs_send, rs_recv, ret_send, ret_recv,
 ):
     width = tokens.shape[1]
@@ -60,11 +62,6 @@
     def beside(c, d):
         return {"dp": near[0][d] + c * (near[1][d] - near[0][d])}
 
-    load_in = pltpu.make_async_copy(w_in_hbm, w_in, load_sem.at[0])
-    load_out = pltpu.make_async_copy(w_out_hbm, w_out, load_sem.at[1])
-    load_in.start()
-    load_out.start()
-
     barrier = pltpu.get_barrier_semaphore()
 
     def greet(k, carry):
@@ -78,6 +75,20 @@
         for d in range(2):
             pl.semaphore_signal(barrier, inc=1, device_id={"dp": near[c][d]}, device_id_type=MESH)
 
+    loads = [
+        pltpu.make_async_copy(source, target, load_sem.at[i])
+        for i, (source, target) in enumerate(
+            (
+                (ids_in, ids), (slots_in, slots), (dropped_in, dropped), (tokens_in, tokens),
+                (gates_in, gates), (out_grad_in, out_grad), (w_in_in, w_in), (w_out_in, w_out),
+            )
+        )
+    ]
+    for load in loads:
+        load.start()
+    for load in loads[:4]:
+        load.wait()
+
     expert = ids[...]
     column = (expert >> 1) * 16 + (expert & 1) * 4 + slots[...]
     column = jnp.where(dropped[...] == 0, column, -64)
@@ -88,7 +99,6 @@
         return jnp.where(mask, 1.0, 0.0).astype(BF16)
 
     chosen = [[onehot(column[k : k + 1, :] + 8 * h == row) for h in range(2)] for k in range(2)]
-    gate = [jnp.broadcast_to(gates[k : k + 1, :], (128, 128)).T[:, :1] for k in range(2)]
     pad = 2 * left - width
 
     def halves(value):
@@ -129,6 +139,9 @@
     pack(0, (token_halves, token_halves))
     pl.semaphore_wait(barrier, N_EXP + 3)
     exchange_start(send, recv, 0, out_way)
+    for load in loads[4:6]:
+        load.wait()
+    gate = [jnp.broadcast_to(gates[k : k + 1, :], (128, 128)).T[:, :1] for k in range(2)]
     pack(1, [halves((gate[k] * out_grad[...].astype(F32)).astype(BF16)) for k in range(2)])
     exchange_start(send, recv, 1, out_way)
 
@@ -136,12 +149,13 @@
     source_row = ((out_row & 31) >> 2) * 16 + (out_row >> 5) * 4 + (out_row & 3)
     shuffle = [onehot(source_row + 8 * h == lane[:64]) for h in range(2)]
 
-    def gather_copy(c, d, a, s):
+    def gather_copy(c, d, a, h, s):
+        rows = pl.ds(h * 16, 16)
         return pltpu.make_async_remote_copy(
-            src_ref=gathered.at[c, a, HALF + 1 - s if d == 0 else HALF - 1 + s],
-            dst_ref=gathered.at[c, a, HALF - s if d == 0 else (HALF + s) % N_DP],
-            send_sem=ag_send.at[c, d, a, s - 1],
-            recv_sem=ag_recv.at[c, d, a, s - 1],
+            src_ref=gathered.at[c, a, HALF + 1 - s if d == 0 else HALF - 1 + s, rows],
+            dst_ref=gathered.at[c, a, HALF - s if d == 0 else (HALF + s) % N_DP, rows],
+            send_sem=ag_send.at[c, d, 2 * a + h, s - 1],
+            recv_sem=ag_recv.at[c, d, 2 * a + h, s - 1],
             device_id=beside(c, d),
             device_id_type=MESH,
         )
@@ -156,9 +170,10 @@
                     gathered[c, a, HALF, :, :left] = block[c * 32 : (c + 1) * 32]
                 else:
                     gathered[c, a, HALF, :, left:] = block[c * 32 : (c + 1) * 32, : width - left]
-        for c in range(2):
-            for d in range(2):
-                gather_copy(c, d, a, 1).start()
+        for h in range(2):
+            for c in range(2):
+                for d in range(2):
+                    gather_copy(c, d, a, h, 1).start()
 
     def experts(c, rows, grads):
         count = rows.shape[0]
@@ -182,12 +197,13 @@
     def sum_slot(d, t):
         return (N_DP + 1 - t) % N_DP if d == 0 else t - 1
 
-    def sum_copy(c, d, a, t):
+    def sum_copy(c, d, a, h, t):
+        rows = pl.ds(h * 16, 16)
         return pltpu.make_async_remote_copy(
-            src_ref=part.at[c, a, sum_slot(d, t)],
-            dst_ref=arrived.at[c, a, N_DP - t if d == 0 else t % HALF],
-            send_sem=rs_send.at[c, d, a, t - 1],
-            recv_sem=rs_recv.at[c, d, a, t - 1],
+            src_ref=part.at[c, a, sum_slot(d, t), rows],
+            dst_ref=arrived.at[c, a, N_DP - t if d == 0 else t % HALF, rows],
+            send_sem=rs_send.at[c, d, 2 * a + h, t - 1],
+            recv_sem=rs_recv.at[c, d, 2 * a + h, t - 1],
             device_id=beside(c, d),
             device_id_type=MESH,
         )
@@ -195,21 +211,19 @@
     def gather_step(s, carry):
         @pl.when(s <= HALF)
         def _():
-            for a in range(2):
-                for c in range(2):
-                    for d in range(2):
-                        gather_copy(c, d, a, s - 1).wait_recv()
-                        if d == a:
-                            gather_copy(c, d, a, s).start()
-                        else:
-                            @pl.when(s < HALF)
-                            def _():
-                                gather_copy(c, d, a, s).start()
+            for a, h, c, d in ORDER:
+                gather_copy(c, d, a, h, s - 1).wait_recv()
+                if d == a:
+                    gather_copy(c, d, a, h, s).start()
+                else:
+                    @pl.when(s < HALF)
+                    def _():
+                        gather_copy(c, d, a, h, s).start()
 
         @pl.when(s == 2)
         def _():
-            load_in.wait()
-            load_out.wait()
+            for load in loads[6:]:
+                load.wait()
 
         c = s % 2
         base = s - 2 - c
@@ -227,34 +241,37 @@
         @pl.when(s >= HALF)
         def _():
             for a in range(2):
-                sum_copy(c, 1 - a, a, 2).start()
+                for h in range(2):
+                    sum_copy(c, 1 - a, a, h, 2).start()
 
         return carry
 
     lax.fori_loop(2, HALF + 2, gather_step, 0)
     for c in range(2):
         for a in range(2):
-            gather_copy(c, a, a, HALF).wait_recv()
+            for h in range(2):
+                gather_copy(c, a, a, h, HALF).wait_recv()
         keep(c, pl.ds(0, 1), experts(c, gathered[c, 0, 0], gathered[c, 1, 0]), 0)
         for a in range(2):
-            sum_copy(c, a, a, 1).start()
-
-    def add(c, d, a, t):
-        sum_copy(c, d, a, t - 1).wait_recv()
-        slot = sum_slot(d, t)
-        part[c, a, slot] = (part[c, a, slot].astype(F32) + arrived[c, a, slot].astype(F32)).astype(BF16)
-        sum_copy(c, d, a, t).start()
+            for h in range(2):
+                sum_copy(c, a, a, h, 1).start()
+
+    def add(c, d, a, h, t):
+        sum_copy(c, d, a, h, t - 1).wait_recv()
+        at = (c, a, sum_slot(d, t), pl.ds(h * 16, 16))
+        part[at] = (part[at].astype(F32) + arrived[at].astype(F32)).astype(BF16)
+        sum_copy(c, d, a, h, t).start()
 
     def sum_step(t, carry):
-        for c in range(2):
-            for a in range(2):
+        for a, h, c, d in ORDER:
+            if d != a:
                 @pl.when(t < HALF)
                 def _():
-                    add(c, 1 - a, a, t + 1)
-
-        for c in range(2):
-            for a in range(2):
-                add(c, a, a, t)
+                    add(c, d, a, h, t + 1)
+
+        for a, h, c, d in ORDER:
+            if d == a:
+                add(c, d, a, h, t)
 
         @pl.when(t <= width // 128 + 1)
         def _():
@@ -275,7 +292,8 @@
         total = []
         for c in range(2):
             for d in range(2):
-                sum_copy(c, d, a, HALF).wait_recv()
+                for h in range(2):
+                    sum_copy(c, d, a, h, HALF).wait_recv()
             total.append(
                 (
                     part[c, a, HALF].astype(F32)
@@ -289,17 +307,15 @@
         exchange_start(send, back, a, home)
 
     def drain(s, carry):
-        for c in range(2):
-            for d in range(2):
-                for a in range(2):
-                    if d == a:
-                        gather_copy(c, d, a, s).wait_send()
-                        sum_copy(c, d, a, s).wait_send()
-                    else:
-                        @pl.when(s < HALF)
-                        def _():
-                            gather_copy(c, d, a, s).wait_send()
-                            sum_copy(c, d, a, s + 1).wait_send()
+        for a, h, c, d in ORDER:
+            if d == a:
+                gather_copy(c, d, a, h, s).wait_send()
+                sum_copy(c, d, a, h, s).wait_send()
+            else:
+                @pl.when(s < HALF)
+                def _():
+                    gather_copy(c, d, a, h, s).wait_send()
+                    sum_copy(c, d, a, h, s + 1).wait_send()
         return carry
 
     lax.fori_loop(1, HALF + 1, drain, 0)
@@ -320,16 +336,30 @@
     tok_grad[...] = (unpack(1, 0) + unpack(1, 1)).astype(BF16)
 
 
+def write_back(*refs):
+    sems = refs[-1]
+    copies = []
+    for i in (3, 4, 0, 1, 2):
+        source, target = refs[i], refs[5 + i]
+        if len(source.shape) == 3:
+            copies += [pltpu.make_async_copy(source.at[c], target.at[c], sems.at[i, c]) for c in range(2)]
+        else:
+            copies.append(pltpu.make_async_copy(source, target, sems.at[i, 0]))
+    for copy in copies:
+        copy.start()
+    for copy in copies:
+        copy.wait()
+
+
 def per_device(tokens, expert_ids, slot_ids, dropped, gates, w_in, w_out, out_grad):
     count, width = tokens.shape
     hidden_units = w_in.shape[2]
-    vmem = pl.BlockSpec(memory_space=pltpu.VMEM)
     anywhere = pl.BlockSpec(memory_space=pl.ANY)
     blocks = pltpu.VMEM((2, 2, N_DP, 32, width), BF16)
     units = pltpu.VMEM((2, N_DP, 32, hidden_units), BF16)
     small = pltpu.VMEM((2, N_EXP, 16, (width // 128 + 1) // 2 * 128), BF16)
     dma = pltpu.SemaphoreType.DMA
-    mixed, tok_grad, gate_grad, w_in_grad, w_out_grad = pl.pallas_call(
+    results = pl.pallas_call(
         kernel,
         out_shape=(
             pltpu.VMEM((count, width), BF16),
@@ -338,13 +368,16 @@
             pltpu.VMEM(w_in.shape, F32),
             pltpu.VMEM(w_out.shape, F32),
         ),
-        in_specs=[vmem] * 6 + [anywhere] * 2,
+        in_specs=[anywhere] * 8,
         scratch_shapes=[
-            blocks, blocks, blocks, units, units,
+            pltpu.VMEM((count, width), BF16),
+            *[pltpu.VMEM((2, count), jnp.int32)] * 3,
+            pltpu.VMEM((2, count), F32),
+            pltpu.VMEM((count, width), BF16),
             pltpu.VMEM(w_in.shape, BF16), pltpu.VMEM(w_out.shape, BF16),
-            small, small, small,
-            dma((2,)), dma((2, N_EXP)), dma((2, N_EXP)),
-            dma((2, 2, 2, HALF)), dma((2, 2, 2, HALF)), dma((2, 2, 2, HALF)), dma((2, 2, 2, HALF)),
+            blocks, blocks, blocks, units, units, small, small, small,
+            dma((8,)), dma((2, N_EXP)), dma((2, N_EXP)),
+            *[dma((2, 2, 4, HALF))] * 4,
             dma((2, N_EXP)), dma((2, N_EXP)),
         ],
         compiler_params=pltpu.CompilerParams(
@@ -354,6 +387,14 @@
             flops=12 * 2048 * width * hidden_units, bytes_accessed=20_000_000, transcendentals=2_000_000
         ),
     )(tokens, expert_ids.T, slot_ids.T, dropped.T, gates.T, out_grad, w_in, w_out)
+    mixed, tok_grad, gate_grad, w_in_grad, w_out_grad = pl.pallas_call(
+        write_back,
+        out_shape=[jax.ShapeDtypeStruct(v.shape, v.dtype) for v in results],
+        in_specs=[anywhere] * 5,
+        out_specs=[anywhere] * 5,
+        scratch_shapes=[dma((5, 2))],
+        compiler_params=pltpu.CompilerParams(vmem_limit_bytes=1024 * 1024),
+    )(*results)
     return mixed, tok_grad, gate_grad.T, w_in_grad, w_out_grad
 
 

time: 193 us -> 188 us (0.974)
  local copies, waits for them, and re-layouts: 5.58 us -> 0 us
    unnamed x5 -> x0, local copies, waits for them, and re-layouts: 5.58 us -> none
    pallas_call x0 -> x1, Pallas kernels: none -> 3.17 us  [per_device(): pl.pallas_call(write_back, out_shape=[jax.ShapeDtypeStruct(v.shape, v.dty...]
    pallas_call x1, Pallas kernels: 186 us -> 184 us  [per_device(): pl.pallas_call(kernel, out_shape=(pltpu.VMEM((count, width), BF16), pltpu...]
where the time goes in v3:
time: 188 us
  Pallas kernels  187 us (99%)
    pallas_call x1, Pallas kernels, per_device(): pl.pallas_call(kernel, out_shape=(pltpu.VMEM((count, width), BF16), pltpu...  184 us

profile of v3, /device:TPU:1, one launch (start us, length us, event | category | flops | bytes accessed | tf_op | source)
XLA Modules:
  0.0 187.9 jit_solution(455355673302888180)
XLA Ops:
  0.6 184.1 %shard_map.119 = (bf16[128,1664]{1,0:T(8,128)(2,1)S(1)}, bf16[128,1664]{1,0:T(8,128)(2,1)S(1)}, f32[2,128]{1,0:T(2,128)S(1)}, f32[2,1664,256]{2,1,0:T(8,128)S(1)}, f32[2,256,1664]{2,1,0:T(8,128)S(1)}) custom-call(bf16[128,1664]{1,0:T(8,128)(2,1)} %tokens_in.1, s32[2,128]{1,0:T(2,128)} %bitcast.5, s32[2,128]{1,0:T(2,128)} %bitcast.6, s32[2,128]{1,0:T(2,128)} %bitcast.7, ...), custom_call_target="tpu_custom_call" | custom-call | flops 10468982784 | bytes 20000000 | tf_op jit(solution)/shard_map/pallas_call | solution.py:362
  184.7 3.2 %shard_map.120 = (bf16[128,1664]{1,0:T(8,128)(2,1)}, bf16[128,1664]{1,0:T(8,128)(2,1)}, f32[2,128]{1,0:T(2,128)}, f32[2,1664,256]{2,1,0:T(8,128)}, f32[2,256,1664]{2,1,0:T(8,128)}) custom-call(bf16[128,1664]{1,0:T(8,128)(2,1)S(1)} %get-tuple-element.15.refs_0_, bf16[128,1664]{1,0:T(8,128)(2,1)S(1)} %get-tuple-element.16.refs_1_, ...), custom_call_target="tpu_custom_call" | custom-call | tf_op jit(solution)/shard_map/pallas_call | solution.py:390

commit v4 on v3

--- a/solution.py
+++ b/solution.py
@@ -98,16 +98,16 @@
     def onehot(mask):
         return jnp.where(mask, 1.0, 0.0).astype(BF16)
 
-    chosen = [[onehot(column[k : k + 1, :] + 8 * h == row) for h in range(2)] for k in range(2)]
-    pad = 2 * left - width
-
-    def halves(value):
-        zeros = jnp.zeros((value.shape[0], pad), BF16)
-        return value[:, :left], jnp.concatenate([value[:, left:], zeros], axis=1)
-
-    def pack(a, values):
-        packed = sum(dot(chosen[k][h], values[k][h], 1, 0) for k in range(2) for h in range(2))
-        send[a] = packed.astype(BF16).reshape(N_EXP, 16, left)
+    def cut(value):
+        zeros = jnp.zeros((value.shape[0], 2 * left - width), BF16)
+        return [value[:, :left], jnp.concatenate([value[:, left:], zeros], axis=1)]
+
+    chosen = [[column[k : k + 1, :] + 8 * h == row for h in range(2)] for k in range(2)]
+    either = [chosen[0][h] | chosen[1][h] for h in range(2)]
+
+    def pack(a, masks, values):
+        masks = jnp.concatenate([onehot(mask) for mask in masks], axis=1)
+        send[a] = dot(masks, jnp.concatenate(values), 1, 0).astype(BF16).reshape(N_EXP, 16, left)
 
     def across(source, target, a, k, sems):
         return pltpu.make_async_remote_copy(
@@ -119,30 +119,26 @@
             device_id_type=MESH,
         )
 
+    far_first = (4, 3, 5, 2, 6, 1, 7)
+
     def exchange_start(source, target, a, sems):
-        def go(k, carry):
+        for k in far_first:
             across(source, target, a, k, sems).start()
-            return carry
-
-        lax.fori_loop(1, N_EXP, go, 0)
         target[a, me_e] = source[a, me_e]
 
     def exchange_wait(source, target, a, sems):
-        def done(k, carry):
+        for k in reversed(far_first):
             across(source, target, a, k, sems).wait()
-            return carry
-
-        lax.fori_loop(1, N_EXP, done, 0)
 
     out_way = (a2a_send, a2a_recv)
-    token_halves = halves(tokens[...])
-    pack(0, (token_halves, token_halves))
+    pack(0, either, cut(tokens[...]))
     pl.semaphore_wait(barrier, N_EXP + 3)
     exchange_start(send, recv, 0, out_way)
     for load in loads[4:6]:
         load.wait()
     gate = [jnp.broadcast_to(gates[k : k + 1, :], (128, 128)).T[:, :1] for k in range(2)]
-    pack(1, [halves((gate[k] * out_grad[...].astype(F32)).astype(BF16)) for k in range(2)])
+    scaled = [cut((gate[k] * out_grad[...].astype(F32)).astype(BF16)) for k in range(2)]
+    pack(1, chosen[0] + chosen[1], scaled[0] + scaled[1])
     exchange_start(send, recv, 1, out_way)
 
     out_row = row[:64]
@@ -175,6 +171,15 @@
                 for d in range(2):
                     gather_copy(c, d, a, h, 1).start()
 
+    def turned(mask):
+        return jnp.where(mask, 1.0, 0.0).T.astype(BF16)
+
+    take = [[turned(chosen[k][h]) for h in range(2)] for k in range(2)]
+    take_either = [turned(either[h]) for h in range(2)]
+    block_row = lane & 63
+    back_row = ((block_row & 31) >> 2) * 16 + (block_row >> 5) * 4 + (block_row & 3) + (lane >> 6) * 8
+    unshuffle = onehot(back_row == row)
+
     def experts(c, rows, grads):
         count = rows.shape[0]
         pre = dot(rows, w_in[c], 1, 0)
@@ -262,51 +267,7 @@
         part[at] = (part[at].astype(F32) + arrived[at].astype(F32)).astype(BF16)
         sum_copy(c, d, a, h, t).start()
 
-    def sum_step(t, carry):
-        for a, h, c, d in ORDER:
-            if d != a:
-                @pl.when(t < HALF)
-                def _():
-                    add(c, d, a, h, t + 1)
-
-        for a, h, c, d in ORDER:
-            if d == a:
-                add(c, d, a, h, t)
-
-        @pl.when(t <= width // 128 + 1)
-        def _():
-            cut = pl.ds(pl.multiple_of((t - 2) * 128, 128), 128)
-            for c in range(2):
-                w_in_grad[c, cut, :] = dot(
-                    gathered[c, 0, :, :, cut].reshape(1024, 128), pre_grad[c].reshape(1024, -1), 0, 0
-                )
-                w_out_grad[c, :, cut] = dot(
-                    hidden[c].reshape(1024, -1), gathered[c, 1, :, :, cut].reshape(1024, 128), 0, 0
-                )
-
-        return carry
-
-    lax.fori_loop(2, HALF + 1, sum_step, 0)
-    home = (ret_send, ret_recv)
-    for a in range(2):
-        total = []
-        for c in range(2):
-            for d in range(2):
-                for h in range(2):
-                    sum_copy(c, d, a, h, HALF).wait_recv()
-            total.append(
-                (
-                    part[c, a, HALF].astype(F32)
-                    + arrived[c, a, HALF].astype(F32)
-                    + arrived[c, a, 0].astype(F32)
-                ).astype(BF16)
-            )
-        total = halves(jnp.concatenate(total))
-        packed = sum(dot(shuffle[h], total[h], 0, 0) for h in range(2))
-        send[a] = packed.astype(BF16).reshape(N_EXP, 16, left)
-        exchange_start(send, back, a, home)
-
-    def drain(s, carry):
+    def sent(s):
         for a, h, c, d in ORDER:
             if d == a:
                 gather_copy(c, d, a, h, s).wait_send()
@@ -316,24 +277,64 @@
                 def _():
                     gather_copy(c, d, a, h, s).wait_send()
                     sum_copy(c, d, a, h, s + 1).wait_send()
+
+    def sum_step(t, carry):
+        for array in range(2):
+            for a, h, c, d in ORDER:
+                if a == array and d != a:
+                    @pl.when(t < HALF)
+                    def _():
+                        add(c, d, a, h, t + 1)
+
+            for a, h, c, d in ORDER:
+                if a == array and d == a:
+                    add(c, d, a, h, t)
+
+        @pl.when(t <= width // 128 + 1)
+        def _():
+            part_of = pl.ds(pl.multiple_of((t - 2) * 128, 128), 128)
+            for c in range(2):
+                w_in_grad[c, part_of, :] = dot(
+                    gathered[c, 0, :, :, part_of].reshape(1024, 128), pre_grad[c].reshape(1024, -1), 0, 0
+                )
+                w_out_grad[c, :, part_of] = dot(
+                    hidden[c].reshape(1024, -1), gathered[c, 1, :, :, part_of].reshape(1024, 128), 0, 0
+                )
+
+        sent(t - 1)
         return carry
 
-    lax.fori_loop(1, HALF + 1, drain, 0)
-
-    def unpack(a, k):
-        returned = back[a].reshape(128, left)
-        first, second = (dot(chosen[k][h], returned, 0, 0) for h in range(2))
-        return jnp.concatenate([first, second[:, : width - left]], axis=1)
-
+    lax.fori_loop(2, HALF + 1, sum_step, 0)
+    home = (ret_send, ret_recv)
+    for a in range(2):
+        total = []
+        for c in range(2):
+            for d in range(2):
+                for h in range(2):
+                    sum_copy(c, d, a, h, HALF).wait_recv()
+            at = part[c, a, HALF].astype(F32) + arrived[c, a, HALF].astype(F32)
+            total.append((at + arrived[c, a, 0].astype(F32)).astype(BF16))
+        total = jnp.concatenate(cut(jnp.concatenate(total)))
+        send[a] = dot(unshuffle, total, 1, 0).astype(BF16).reshape(N_EXP, 16, left)
+        exchange_start(send, back, a, home)
+    sent(HALF)
+
+    spans = (pl.ds(0, left), pl.ds(left, width - left))
     exchange_wait(send, back, 0, home)
-    grad_wide = out_grad[...].astype(F32)
-    picked = [unpack(0, k) for k in range(2)]
-    mixed[...] = (gate[0] * picked[0] + gate[1] * picked[1]).astype(BF16)
+    returned = back[0].reshape(128, left)
+    inner = [0.0, 0.0]
+    for h in range(2):
+        picked = [dot(take[k][h], returned[:, : spans[h].size], 1, 0) for k in range(2)]
+        mixed[:, spans[h]] = (gate[0] * picked[0] + gate[1] * picked[1]).astype(BF16)
+        grad_wide = out_grad[:, spans[h]].astype(F32)
+        for k in range(2):
+            inner[k] += jnp.sum(picked[k] * grad_wide, axis=1, keepdims=True)
     for k in range(2):
-        inner = jnp.sum(picked[k] * grad_wide, axis=1, keepdims=True)
-        gate_grad[k : k + 1, :] = jnp.broadcast_to(inner, (128, 128)).T[:1]
+        gate_grad[k : k + 1, :] = jnp.broadcast_to(inner[k], (128, 128)).T[:1]
     exchange_wait(send, back, 1, home)
-    tok_grad[...] = (unpack(1, 0) + unpack(1, 1)).astype(BF16)
+    returned = back[1].reshape(128, left)
+    for h in range(2):
+        tok_grad[:, spans[h]] = dot(take_either[h], returned[:, : spans[h].size], 1, 0).astype(BF16)
 
 
 def write_back(*refs):

time: 188 us -> 187 us (level)
  no operation moved by 1% of the time
where the time goes in v4:
time: 187 us; the launch traced here: 186 us
  Pallas kernels  186 us (99%)
    pallas_call x1, Pallas kernels, per_device(): pl.pallas_call(kernel, out_shape=(pltpu.VMEM((count, width), BF16), pltpu...  183 us

profile of v4, /device:TPU:1, one launch (start us, length us, event | category | flops | bytes accessed | tf_op | source)
XLA Modules:
  0.0 186.5 jit_solution(5479115483599454752)
XLA Ops:
  0.6 182.7 %shard_map.119 = (bf16[128,1664]{1,0:T(8,128)(2,1)S(1)}, bf16[128,1664]{1,0:T(8,128)(2,1)S(1)}, f32[2,128]{1,0:T(2,128)S(1)}, f32[2,1664,256]{2,1,0:T(8,128)S(1)}, f32[2,256,1664]{2,1,0:T(8,128)S(1)}) custom-call(bf16[128,1664]{1,0:T(8,128)(2,1)} %tokens_in.1, s32[2,128]{1,0:T(2,128)} %bitcast.5, s32[2,128]{1,0:T(2,128)} %bitcast.6, s32[2,128]{1,0:T(2,128)} %bitcast.7, ...), custom_call_target="tpu_custom_call" | custom-call | flops 10468982784 | bytes 20000000 | tf_op jit(solution)/shard_map/pallas_call | solution.py:363
  183.3 3.2 %shard_map.120 = (bf16[128,1664]{1,0:T(8,128)(2,1)}, bf16[128,1664]{1,0:T(8,128)(2,1)}, f32[2,128]{1,0:T(2,128)}, f32[2,1664,256]{2,1,0:T(8,128)}, f32[2,256,1664]{2,1,0:T(8,128)}) custom-call(bf16[128,1664]{1,0:T(8,128)(2,1)S(1)} %get-tuple-element.15.refs_0_, bf16[128,1664]{1,0:T(8,128)(2,1)S(1)} %get-tuple-element.16.refs_1_, ...), custom_call_target="tpu_custom_call" | custom-call | tf_op jit(solution)/shard_map/pallas_call | solution.py:391

commit v5 on v4

--- a/solution.py
+++ b/solution.py
@@ -9,6 +9,7 @@
 N_EXP = 8
 N_DP = 32
 HALF = 16
+TURNS = 8
 BF16 = jnp.bfloat16
 F32 = jnp.float32
 MESH = pl.DeviceIdType.MESH
@@ -48,7 +49,7 @@
     mixed, tok_grad, gate_grad, w_in_grad, w_out_grad,
     tokens, ids, slots, dropped, gates, out_grad, w_in, w_out,
     gathered, part, arrived, hidden, pre_grad, send, recv, back,
-    load_sem, a2a_send, a2a_recv, ag_send, ag_recv, rs_send, rs_recv, ret_send, ret_recv,
+    load_sem, a2a_send, a2a_recv, ret_recv, ring_send, ring_recv,
 ):
     width = tokens.shape[1]
     left = send.shape[3]
@@ -150,8 +151,8 @@
         return pltpu.make_async_remote_copy(
             src_ref=gathered.at[c, a, HALF + 1 - s if d == 0 else HALF - 1 + s, rows],
             dst_ref=gathered.at[c, a, HALF - s if d == 0 else (HALF + s) % N_DP, rows],
-            send_sem=ag_send.at[c, d, 2 * a + h, s - 1],
-            recv_sem=ag_recv.at[c, d, 2 * a + h, s - 1],
+            send_sem=ring_send.at[c, d, 2 * a + h, s % 2],
+            recv_sem=ring_recv.at[c, d, 2 * a + h, s % TURNS],
             device_id=beside(c, d),
             device_id_type=MESH,
         )
@@ -207,23 +208,32 @@
         return pltpu.make_async_remote_copy(
             src_ref=part.at[c, a, sum_slot(d, t), rows],
             dst_ref=arrived.at[c, a, N_DP - t if d == 0 else t % HALF, rows],
-            send_sem=rs_send.at[c, d, 2 * a + h, t - 1],
-            recv_sem=rs_recv.at[c, d, 2 * a + h, t - 1],
+            send_sem=ring_send.at[c, d, 2 * a + h, t % 2],
+            recv_sem=ring_recv.at[c, d, 2 * a + h, t % TURNS],
             device_id=beside(c, d),
             device_id_type=MESH,
         )
+
+    def after_last(copy):
+        copy.wait_send()
+        copy.start()
 
     def gather_step(s, carry):
         @pl.when(s <= HALF)
         def _():
             for a, h, c, d in ORDER:
                 gather_copy(c, d, a, h, s - 1).wait_recv()
-                if d == a:
+
+                @pl.when(s > 2)
+                def _():
+                    if d == a:
+                        after_last(gather_copy(c, d, a, h, s))
+                    else:
+                        pl.when(s < HALF)(lambda: after_last(gather_copy(c, d, a, h, s)))
+
+                @pl.when(s == 2)
+                def _():
                     gather_copy(c, d, a, h, s).start()
-                else:
-                    @pl.when(s < HALF)
-                    def _():
-                        gather_copy(c, d, a, h, s).start()
 
         @pl.when(s == 2)
         def _():
@@ -247,7 +257,7 @@
         def _():
             for a in range(2):
                 for h in range(2):
-                    sum_copy(c, 1 - a, a, h, 2).start()
+                    after_last(sum_copy(c, 1 - a, a, h, 2))
 
         return carry
 
@@ -259,24 +269,13 @@
         keep(c, pl.ds(0, 1), experts(c, gathered[c, 0, 0], gathered[c, 1, 0]), 0)
         for a in range(2):
             for h in range(2):
-                sum_copy(c, a, a, h, 1).start()
+                after_last(sum_copy(c, a, a, h, 1))
 
     def add(c, d, a, h, t):
         sum_copy(c, d, a, h, t - 1).wait_recv()
         at = (c, a, sum_slot(d, t), pl.ds(h * 16, 16))
         part[at] = (part[at].astype(F32) + arrived[at].astype(F32)).astype(BF16)
-        sum_copy(c, d, a, h, t).start()
-
-    def sent(s):
-        for a, h, c, d in ORDER:
-            if d == a:
-                gather_copy(c, d, a, h, s).wait_send()
-                sum_copy(c, d, a, h, s).wait_send()
-            else:
-                @pl.when(s < HALF)
-                def _():
-                    gather_copy(c, d, a, h, s).wait_send()
-                    sum_copy(c, d, a, h, s + 1).wait_send()
+        after_last(sum_copy(c, d, a, h, t))
 
     def sum_step(t, carry):
         for array in range(2):
@@ -301,11 +300,10 @@
                     hidden[c].reshape(1024, -1), gathered[c, 1, :, :, part_of].reshape(1024, 128), 0, 0
                 )
 
-        sent(t - 1)
         return carry
 
     lax.fori_loop(2, HALF + 1, sum_step, 0)
-    home = (ret_send, ret_recv)
+    home = (a2a_send, ret_recv)
     for a in range(2):
         total = []
         for c in range(2):
@@ -317,7 +315,9 @@
         total = jnp.concatenate(cut(jnp.concatenate(total)))
         send[a] = dot(unshuffle, total, 1, 0).astype(BF16).reshape(N_EXP, 16, left)
         exchange_start(send, back, a, home)
-    sent(HALF)
+    for a, h, c, d in ORDER:
+        for t in (HALF - 1, HALF):
+            sum_copy(c, d, a, h, t).wait_send()
 
     spans = (pl.ds(0, left), pl.ds(left, width - left))
     exchange_wait(send, back, 0, home)
@@ -377,9 +377,8 @@
             pltpu.VMEM((count, width), BF16),
             pltpu.VMEM(w_in.shape, BF16), pltpu.VMEM(w_out.shape, BF16),
             blocks, blocks, blocks, units, units, small, small, small,
-            dma((8,)), dma((2, N_EXP)), dma((2, N_EXP)),
-            *[dma((2, 2, 4, HALF))] * 4,
-            dma((2, N_EXP)), dma((2, N_EXP)),
+            dma((8,)), dma((2, N_EXP)), dma((2, N_EXP)), dma((2, N_EXP)),
+            dma((2, 2, 4, 2)), dma((2, 2, 4, TURNS)),
         ],
         compiler_params=pltpu.CompilerParams(
             collective_id=0, has_side_effects=True, vmem_limit_bytes=50 * 1024 * 1024

time: 187 us -> 179 us (0.957)
  Pallas kernels: 186 us -> 178 us
    pallas_call x1, Pallas kernels: 183 us -> 175 us  [per_device(): pl.pallas_call(kernel, out_shape=(pltpu.VMEM((count, width), BF16), pltpu...]
where the time goes in v5:
time: 179 us
  Pallas kernels  178 us (99%)
    pallas_call x1, Pallas kernels, per_device(): pl.pallas_call(kernel, out_shape=(pltpu.VMEM((count, width), BF16), pltpu...  175 us

profile of v5, /device:TPU:1, one launch (start us, length us, event | category | flops | bytes accessed | tf_op | source)
XLA Modules:
  0.0 178.7 jit_solution(5819172917109274596)
XLA Ops:
  0.6 174.8 %shard_map.119 = (bf16[128,1664]{1,0:T(8,128)(2,1)S(1)}, bf16[128,1664]{1,0:T(8,128)(2,1)S(1)}, f32[2,128]{1,0:T(2,128)S(1)}, f32[2,1664,256]{2,1,0:T(8,128)S(1)}, f32[2,256,1664]{2,1,0:T(8,128)S(1)}) custom-call(bf16[128,1664]{1,0:T(8,128)(2,1)} %tokens_in.1, s32[2,128]{1,0:T(2,128)} %bitcast.5, s32[2,128]{1,0:T(2,128)} %bitcast.6, s32[2,128]{1,0:T(2,128)} %bitcast.7, ...), custom_call_target="tpu_custom_call" | custom-call | flops 10468982784 | bytes 20000000 | tf_op jit(solution)/shard_map/pallas_call | solution.py:363
  175.5 3.2 %shard_map.120 = (bf16[128,1664]{1,0:T(8,128)(2,1)}, bf16[128,1664]{1,0:T(8,128)(2,1)}, f32[2,128]{1,0:T(2,128)}, f32[2,1664,256]{2,1,0:T(8,128)}, f32[2,256,1664]{2,1,0:T(8,128)}) custom-call(bf16[128,1664]{1,0:T(8,128)(2,1)S(1)} %get-tuple-element.15.refs_0_, bf16[128,1664]{1,0:T(8,128)(2,1)S(1)} %get-tuple-element.16.refs_1_, ...), custom_call_target="tpu_custom_call" | custom-call | tf_op jit(solution)/shard_map/pallas_call | solution.py:390

commit v6 on v5

--- a/solution.py
+++ b/solution.py
@@ -226,7 +226,7 @@
 
                 @pl.when(s > 2)
                 def _():
-                    if d == a:
+                    if d == h:
                         after_last(gather_copy(c, d, a, h, s))
                     else:
                         pl.when(s < HALF)(lambda: after_last(gather_copy(c, d, a, h, s)))
@@ -257,7 +257,7 @@
         def _():
             for a in range(2):
                 for h in range(2):
-                    after_last(sum_copy(c, 1 - a, a, h, 2))
+                    after_last(sum_copy(c, 1 - h, a, h, 2))
 
         return carry
 
@@ -265,11 +265,11 @@
     for c in range(2):
         for a in range(2):
             for h in range(2):
-                gather_copy(c, a, a, h, HALF).wait_recv()
+                gather_copy(c, h, a, h, HALF).wait_recv()
         keep(c, pl.ds(0, 1), experts(c, gathered[c, 0, 0], gathered[c, 1, 0]), 0)
         for a in range(2):
             for h in range(2):
-                after_last(sum_copy(c, a, a, h, 1))
+                after_last(sum_copy(c, h, a, h, 1))
 
     def add(c, d, a, h, t):
         sum_copy(c, d, a, h, t - 1).wait_recv()
@@ -280,13 +280,13 @@
     def sum_step(t, carry):
         for array in range(2):
             for a, h, c, d in ORDER:
-                if a == array and d != a:
+                if a == array and d != h:
                     @pl.when(t < HALF)
                     def _():
                         add(c, d, a, h, t + 1)
 
             for a, h, c, d in ORDER:
-                if a == array and d == a:
+                if a == array and d == h:
                     add(c, d, a, h, t)
 
         @pl.when(t <= width // 128 + 1)
@@ -343,7 +343,10 @@
     for i in (3, 4, 0, 1, 2):
         source, target = refs[i], refs[5 + i]
         if len(source.shape) == 3:
-            copies += [pltpu.make_async_copy(source.at[c], target.at[c], sems.at[i, c]) for c in range(2)]
+            size = source.shape[1] // 2
+            for q in range(4):
+                at = (q // 2, pl.ds(q % 2 * size, size))
+                copies.append(pltpu.make_async_copy(source.at[at], target.at[at], sems.at[i, q]))
         else:
             copies.append(pltpu.make_async_copy(source, target, sems.at[i, 0]))
     for copy in copies:
@@ -392,7 +395,7 @@
         out_shape=[jax.ShapeDtypeStruct(v.shape, v.dtype) for v in results],
         in_specs=[anywhere] * 5,
         out_specs=[anywhere] * 5,
-        scratch_shapes=[dma((5, 2))],
+        scratch_shapes=[dma((5, 4))],
         compiler_params=pltpu.CompilerParams(vmem_limit_bytes=1024 * 1024),
     )(*results)
     return mixed, tok_grad, gate_grad.T, w_in_grad, w_out_grad

time: 179 us -> 176 us (0.983)
  Pallas kernels: 178 us -> 175 us
    pallas_call x1, Pallas kernels: 175 us -> 172 us  [per_device(): pl.pallas_call(kernel, out_shape=(pltpu.VMEM((count, width), BF16), pltpu...]
where the time goes in v6:
time: 176 us; the launch traced here: 175 us
  Pallas kernels  175 us (99%)
    pallas_call x1, Pallas kernels, per_device(): pl.pallas_call(kernel, out_shape=(pltpu.VMEM((count, width), BF16), pltpu...  172 us

profile of v6, /device:TPU:1, one launch (start us, length us, event | category | flops | bytes accessed | tf_op | source)
XLA Modules:
  0.0 175.4 jit_solution(14269441149178963932)
XLA Ops:
  0.6 171.6 %shard_map.119 = (bf16[128,1664]{1,0:T(8,128)(2,1)S(1)}, bf16[128,1664]{1,0:T(8,128)(2,1)S(1)}, f32[2,128]{1,0:T(2,128)S(1)}, f32[2,1664,256]{2,1,0:T(8,128)S(1)}, f32[2,256,1664]{2,1,0:T(8,128)S(1)}) custom-call(bf16[128,1664]{1,0:T(8,128)(2,1)} %tokens_in.1, s32[2,128]{1,0:T(2,128)} %bitcast.5, s32[2,128]{1,0:T(2,128)} %bitcast.6, s32[2,128]{1,0:T(2,128)} %bitcast.7, ...), custom_call_target="tpu_custom_call" | custom-call | flops 10468982784 | bytes 20000000 | tf_op jit(solution)/shard_map/pallas_call | solution.py:366
  172.2 3.2 %shard_map.120 = (bf16[128,1664]{1,0:T(8,128)(2,1)}, bf16[128,1664]{1,0:T(8,128)(2,1)}, f32[2,128]{1,0:T(2,128)}, f32[2,1664,256]{2,1,0:T(8,128)}, f32[2,256,1664]{2,1,0:T(8,128)}) custom-call(bf16[128,1664]{1,0:T(8,128)(2,1)S(1)} %get-tuple-element.15.refs_0_, bf16[128,1664]{1,0:T(8,128)(2,1)S(1)} %get-tuple-element.16.refs_1_, ...), custom_call_target="tpu_custom_call" | custom-call | tf_op jit(solution)/shard_map/pallas_call | solution.py:393
